TPU v7x, 256 devices: a whole 4x4x8 slice. The times are simulated.
256 devices in a mesh: dp: 4 (over x), segment: 2 (over core), band: 32 (over z, y).
Axes of the slice: x: 4, y: 4, z: 8, core: 2. Of those that a mesh axis runs over, the one named last changes fastest.
Arguments:
- fields: bfloat16 [4, 2, 256, 16, 512], P('dp', None, 'band'), may hold values from -6 to 6
- cell_mask: int32 [4, 2, 256, 16], P('dp', None, 'band'), may hold values 0 or 1
- merge_weight: bfloat16 [2, 1024, 512], P('segment', 'dp'), may hold values from -0.1875 to 0.1875
- qkv_weight: bfloat16 [2, 512, 1536], P('segment', 'dp')
- out_weight: bfloat16 [2, 512, 512], P('segment', 'dp'), may hold values from -1 to 1
- norm_gain: bfloat16 [2, 512], P('segment', 'dp'), may hold values from 0.099609375 to 1.8984375
- out_cotangent: bfloat16 [4, 2, 256, 16, 512], P('dp', None, 'band'), may hold values from -6 to 6
Outputs:
- section_out: bfloat16 [2, 4, 2, 256, 16, 512], P('segment', 'dp', None, 'band')
- merge_grad: float32 [2, 1024, 512], P('segment', 'dp')
- qkv_grad: float32 [2, 512, 1536], P('segment', 'dp')
- out_grad: float32 [2, 512, 512], P('segment', 'dp')
- gain_grad: float32 [2, 512], P('segment', 'dp')
Inputs may be any that keep to these rules, and one draw needn't show every extreme that they name: `cell_mask`: 1 marks a cell whose keys may be attended.
All inputs are finite; a program needn't handle non-finite values. No bound on the sum of `cell_mask` on one device may be relied on, other than what follows from the above.
Results may differ from a plain program's by a relative error of at most 0.03.
Values may be sent and summed in bfloat16 or wider, within the bound.
A program may use at most 128 MiB of HBM per device.

v0:
```python
from functools import partial
import jax
import jax.numpy as jnp
from jax import lax
from jax.sharding import PartitionSpec as P

HEADS = 8
WH = 8
WW = 16
SH = 4
SW = 8
EPSILON = 1e-05
MASKED = -1e30


def padded(shard, sides, width):
    for axis, dim in sides:
        size, length = (lax.axis_size(axis), shard.shape[dim])
        up = [(i, (i + 1) % size) for i in range(size - 1)]
        down = [(j, i) for i, j in up]
        last = lax.slice_in_dim(shard, length - width, length, axis=dim)
        first = lax.slice_in_dim(shard, 0, width, axis=dim)
        before = lax.ppermute(last, axis, up)
        after = lax.ppermute(first, axis, down)
        shard = jnp.concatenate([before, shard, after], axis=dim)
    return shard


def partner(shard, axis, distance):
    return lax.ppermute(shard, axis, [(i, i ^ 1 << distance) for i in range(lax.axis_size(axis))])


def normalize(update):
    average = jnp.mean(update, axis=-1, keepdims=True)
    centered = update - average
    spread = jnp.mean(centered * centered, axis=-1, keepdims=True)
    inverse = lax.rsqrt(spread + EPSILON)
    return (centered * inverse, inverse)


def window_pattern(lon_count):
    query_index = jnp.arange(WH * lon_count, dtype=jnp.int32)
    key_index = jnp.arange(2 * WH * lon_count, dtype=jnp.int32)
    query_row = query_index // lon_count
    query_col = query_index % lon_count
    key_row = key_index // lon_count
    key_col = key_index % lon_count
    lat_same = ((query_row + SH) // WH)[:, None] == (key_row // WH)[None, :]
    lon_same = ((query_col + SW) // WW)[:, None] == ((key_col + SW) // WW)[None, :]
    self_key = ((query_row + SH)[:, None] == key_row[None, :]) & (
        query_col[:, None] == key_col[None, :]
    )
    return (lat_same & lon_same, self_key)


def attend(queries, keyvals, usable):
    row_count, lon_count, feature = queries.shape
    blocks = row_count // WH
    head_dim = feature // HEADS
    query_blocks = queries.reshape(blocks, WH * lon_count, HEADS, head_dim)
    kv_blocks = keyvals.reshape(blocks + 1, WH * lon_count, 2, HEADS, head_dim)
    key_pairs = jnp.concatenate([kv_blocks[:-1], kv_blocks[1:]], axis=1)
    use_blocks = usable.reshape(blocks + 1, WH * lon_count)
    use_pairs = jnp.concatenate([use_blocks[:-1], use_blocks[1:]], axis=1)
    inside, self_key = window_pattern(lon_count)
    allowed = inside[None] & (use_pairs[:, None, :] | self_key[None])
    scores = jnp.einsum(
        "nqhd,nkhd->nhqk", query_blocks, key_pairs[:, :, 0], preferred_element_type=jnp.float32
    ) * head_dim ** (-0.5)
    scores = jnp.where(allowed[:, None], scores, MASKED)
    highest = jnp.max(scores, axis=-1, keepdims=True)
    weights = jnp.exp(scores - highest)
    attn_prob = (weights / jnp.sum(weights, axis=-1, keepdims=True)).astype(jnp.bfloat16)
    mixture = jnp.einsum(
        "nhqk,nkhd->nqhd", attn_prob, key_pairs[:, :, 1], preferred_element_type=jnp.float32
    )
    return mixture.reshape(row_count, lon_count, feature).astype(jnp.bfloat16)


def guarded(active, function, operands):

    def skipped(values):
        return jax.tree.map(jnp.zeros_like, function(values))

    return lax.cond(active, function, skipped, operands)


def project(joined, merge_full, qkv_full, gain_full):
    update = jnp.einsum("rwj,jd->rwd", joined, merge_full, preferred_element_type=jnp.float32)
    normed, inverse = normalize(update)
    hidden = (normed * gain_full.astype(jnp.float32)).astype(jnp.bfloat16)
    projected = jnp.einsum("rwd,de->rwe", hidden, qkv_full, preferred_element_type=jnp.float32)
    feature = update.shape[-1]
    queries = projected[..., :feature].astype(jnp.bfloat16)
    keyvals = projected[..., feature:].astype(jnp.bfloat16)
    return (update, normed, inverse, hidden, queries, keyvals)


def section_forward(active, joined, usable, merge_full, qkv_full, gain_full, out_full):
    update, normed, inverse, hidden, queries, own_keys = guarded(
        active, lambda rows_own: project(rows_own, merge_full, qkv_full, gain_full), joined
    )
    keyvals = padded(own_keys, (("band", 0),), SH)

    def finish(operands):
        update_in, query_in, keyval_in, usable_in = operands
        mixture = attend(query_in, keyval_in, usable_in)
        result = (
            update_in
            + jnp.einsum("rwd,de->rwe", mixture, out_full, preferred_element_type=jnp.float32)
        ).astype(jnp.bfloat16)
        return (mixture, result)

    mixture, result = guarded(active, finish, (update, queries, keyvals, usable))
    return (result, (joined, normed, inverse, hidden, queries, keyvals, mixture))


def attend_back(out_full, operands):
    grad_out, queries, keyvals, mixture, usable = operands
    grad_mixture = jnp.einsum(
        "rwe,de->rwd", grad_out, out_full, preferred_element_type=jnp.float32
    ).astype(jnp.bfloat16)
    unused, pull_back = jax.vjp(
        lambda query_in, keyval_in: attend(query_in, keyval_in, usable), queries, keyvals
    )
    grad_query, grad_keyval = pull_back(grad_mixture)
    grad_outw = jnp.einsum("rwd,rwe->de", mixture, grad_out, preferred_element_type=jnp.float32)
    return (grad_query, grad_keyval, grad_outw)


def fold_rims(grad_keyval, row_count):
    rim_rows = jnp.concatenate([grad_keyval[:SH], grad_keyval[SH + row_count :]], axis=0)
    returned = padded(rim_rows, (("band", 0),), SH)
    own_part = grad_keyval[SH : SH + row_count].astype(jnp.float32)
    return jnp.concatenate(
        [
            own_part[:SH] + returned[:SH].astype(jnp.float32),
            own_part[SH : row_count - SH],
            own_part[row_count - SH :] + returned[3 * SH :].astype(jnp.float32),
        ],
        axis=0,
    ).astype(jnp.bfloat16)


def back_core(qkv_full, gain_full, grad_query, grad_keyown, grad_out, normed, inverse):
    grad_proj = jnp.concatenate([grad_query, grad_keyown], axis=-1)
    grad_hidden = jnp.einsum("rwe,de->rwd", grad_proj, qkv_full, preferred_element_type=jnp.float32)
    grad_normed = grad_hidden * gain_full.astype(jnp.float32)
    grad_update = (
        grad_out.astype(jnp.float32)
        + inverse
        * (
            grad_normed
            - jnp.mean(grad_normed, axis=-1, keepdims=True)
            - normed * jnp.mean(grad_normed * normed, axis=-1, keepdims=True)
        )
    ).astype(jnp.bfloat16)
    return (grad_proj, grad_hidden, grad_update)


def project_back(merge_part, qkv_full, gain_full, operands):
    grad_query, grad_keyown, grad_out, joined, normed, inverse, hidden = operands
    grad_proj, grad_hidden, grad_update = back_core(
        qkv_full, gain_full, grad_query, grad_keyown, grad_out, normed, inverse
    )
    grad_qkv = jnp.einsum("rwd,rwe->de", hidden, grad_proj, preferred_element_type=jnp.float32)
    grad_gain = jnp.sum(grad_hidden * normed, axis=(0, 1))
    grad_merge = jnp.einsum("rwj,rwd->jd", joined, grad_update, preferred_element_type=jnp.float32)
    grad_joined = jnp.einsum(
        "rwd,jd->rwj", grad_update, merge_part, preferred_element_type=jnp.float32
    )
    return (grad_joined, grad_merge, grad_qkv, grad_gain)


def store_slot(buffers, values, slot_index, active):

    def place_one(buffer, new_value):
        current = lax.dynamic_index_in_dim(buffer, slot_index, 0, keepdims=False)
        return lax.dynamic_update_index_in_dim(
            buffer, jnp.where(active, new_value, current), slot_index, 0
        )

    return jax.tree.map(place_one, buffers, values)


def body(fields, cell_mask, merge_weight, qkv_weight, out_weight, norm_gain, out_cotangent):
    merge_rows, qkv_rows, out_rows, gain_rows = (
        lax.all_gather(merge_weight, "dp", axis=1, tiled=True),
        lax.all_gather(qkv_weight, "dp", axis=1, tiled=True),
        lax.all_gather(out_weight, "dp", axis=1, tiled=True),
        lax.all_gather(norm_gain, "dp", axis=1, tiled=True),
    )
    merge_full = merge_rows[0]
    qkv_full = qkv_rows[0]
    out_full = out_rows[0]
    gain_full = gain_rows[0]
    inputs = fields[0]
    cotangent = out_cotangent[0]
    micro_count, row_count, lon_count, feature = inputs.shape
    mask_ext = padded(cell_mask[0], (("band", 1),), SH)
    usable_ext = mask_ext == 1
    section_count = lax.axis_size("segment")
    half_count = section_count // 2
    section_rank = lax.axis_index("segment")
    tick_count = half_count + micro_count - 1

    def to_partner(payload):
        payload = partner(payload, "segment", 0)
        return payload

    def forward_tick(phase, feed):

        def forward_one_tick(tick_index, state_in):
            sending, section_buf, stashed = state_in
            rank_local = section_rank - phase * half_count
            micro_index = tick_index - rank_local
            active = (
                (rank_local >= 0)
                & (rank_local < half_count)
                & (micro_index >= 0)
                & (micro_index < micro_count)
            )
            slot_index = jnp.clip(micro_index, 0, micro_count - 1)
            feed_now = lax.dynamic_index_in_dim(feed, slot_index, 0, keepdims=False)
            joined = jnp.concatenate([feed_now, feed_now], axis=-1)
            usable = lax.dynamic_index_in_dim(usable_ext, slot_index, 0, keepdims=False)
            result, record = section_forward(
                active, joined, usable, merge_full, qkv_full, gain_full, out_full
            )
            section_buf = store_slot(section_buf, result, slot_index, active)
            stashed = store_slot(stashed, record, slot_index, active)
            return (result, section_buf, stashed)

        return forward_one_tick

    def backward_tick(phase, feed, stashed):
        merge_part = merge_full if phase == 0 else merge_full[:feature]

        def backward_one_tick(tick_index, state_in):
            sending, skip_buf, grad_sums = state_in
            rank_local = section_count - 1 - section_rank - phase * half_count
            micro_index = tick_index - rank_local
            active = (
                (rank_local >= 0)
                & (rank_local < half_count)
                & (micro_index >= 0)
                & (micro_index < micro_count)
            )
            slot_index = jnp.clip(micro_index, 0, micro_count - 1)
            grad_out = lax.dynamic_index_in_dim(feed, slot_index, 0, keepdims=False)
            joined, normed, inverse, hidden, queries, keyvals, mixture = jax.tree.map(
                lambda buffer: lax.dynamic_index_in_dim(buffer, slot_index, 0, keepdims=False),
                stashed,
            )
            usable = lax.dynamic_index_in_dim(usable_ext, slot_index, 0, keepdims=False)
            grad_query, grad_keyval, grad_outw = guarded(
                active,
                partial(attend_back, out_full),
                (grad_out, queries, keyvals, mixture, usable),
            )
            grad_keyown = fold_rims(grad_keyval, row_count)
            grad_joined, grad_merge, grad_qkv, grad_gain = guarded(
                active,
                partial(project_back, merge_part, qkv_full, gain_full),
                (grad_query, grad_keyown, grad_out, joined, normed, inverse, hidden),
            )
            grad_sums = (
                grad_sums[0] + grad_merge,
                grad_sums[1] + grad_qkv,
                grad_sums[2] + grad_outw,
                grad_sums[3] + grad_gain,
            )
            grad_chain = grad_joined[..., :feature].astype(jnp.bfloat16)
            if phase == 0:
                grad_side = grad_joined[..., feature:].astype(jnp.bfloat16)
                toward = jnp.where(
                    section_rank == half_count,
                    (grad_chain.astype(jnp.float32) + grad_side.astype(jnp.float32)).astype(
                        jnp.bfloat16
                    ),
                    grad_side,
                )
                skip_buf = store_slot(skip_buf, toward, slot_index, active)
            return (grad_chain, skip_buf, grad_sums)

        return backward_one_tick

    stashed = (
        jnp.zeros((micro_count, row_count, lon_count, 2 * feature), jnp.bfloat16),
        jnp.zeros((micro_count, row_count, lon_count, feature), jnp.float32),
        jnp.zeros((micro_count, row_count, lon_count, 1), jnp.float32),
        jnp.zeros((micro_count, row_count, lon_count, feature), jnp.bfloat16),
        jnp.zeros((micro_count, row_count, lon_count, feature), jnp.bfloat16),
        jnp.zeros((micro_count, row_count + 2 * SH, lon_count, 2 * feature), jnp.bfloat16),
        jnp.zeros((micro_count, row_count, lon_count, feature), jnp.bfloat16),
    )
    section_buf = jnp.zeros((micro_count, row_count, lon_count, feature), jnp.bfloat16)
    spare_rows = jnp.zeros((row_count, lon_count, feature), jnp.bfloat16)
    unused, section_buf, stashed = lax.fori_loop(
        0, tick_count, forward_tick(0, inputs), (spare_rows, section_buf, stashed)
    )
    skip_in = to_partner(section_buf)
    unused, section_buf, stashed = lax.fori_loop(
        0, tick_count, forward_tick(1, skip_in), (spare_rows, section_buf, stashed)
    )
    grad_sums = (
        jnp.zeros((2 * feature, feature), jnp.float32),
        jnp.zeros((feature, 3 * feature), jnp.float32),
        jnp.zeros((feature, feature), jnp.float32),
        jnp.zeros((feature,), jnp.float32),
    )
    unused, skip_buf, grad_sums = lax.fori_loop(
        0,
        tick_count,
        backward_tick(0, cotangent, stashed),
        (spare_rows, jnp.zeros_like(section_buf), grad_sums),
    )
    skip_back = to_partner(skip_buf)
    unused, skip_buf, grad_sums = lax.fori_loop(
        0, tick_count, backward_tick(1, skip_back, stashed), (spare_rows, skip_buf, grad_sums)
    )
    section_home = section_buf[None, None]
    merge_part_sum, qkv_part_sum, out_part_sum, gain_part_sum = (
        lax.psum_scatter(
            grad_sums[0][None].astype(jnp.bfloat16), "dp", scatter_dimension=1, tiled=True
        ).astype(jnp.float32),
        lax.psum_scatter(
            grad_sums[1][None].astype(jnp.bfloat16), "dp", scatter_dimension=1, tiled=True
        ).astype(jnp.float32),
        lax.psum_scatter(
            grad_sums[2][None].astype(jnp.bfloat16), "dp", scatter_dimension=1, tiled=True
        ).astype(jnp.float32),
        lax.psum_scatter(
            grad_sums[3][None].astype(jnp.bfloat16), "dp", scatter_dimension=1, tiled=True
        ).astype(jnp.float32),
    )
    merge_grad, qkv_grad, out_grad, gain_grad = (
        lax.psum(merge_part_sum.astype(jnp.bfloat16), "band").astype(jnp.float32),
        lax.psum(qkv_part_sum.astype(jnp.bfloat16), "band").astype(jnp.float32),
        lax.psum(out_part_sum.astype(jnp.bfloat16), "band").astype(jnp.float32),
        lax.psum(gain_part_sum.astype(jnp.bfloat16), "band").astype(jnp.float32),
    )
    return (section_home, merge_grad, qkv_grad, out_grad, gain_grad)


def solution(mesh):
    return jax.shard_map(
        body,
        mesh=mesh,
        in_specs=(
            P("dp", None, "band", None, None),
            P("dp", None, "band", None),
            P("segment", "dp", None),
            P("segment", "dp", None),
            P("segment", "dp", None),
            P("segment", "dp"),
            P("dp", None, "band", None, None),
        ),
        out_specs=(
            P("segment", "dp", None, "band", None, None),
            P("segment", "dp", None),
            P("segment", "dp", None),
            P("segment", "dp", None),
            P("segment", "dp"),
        ),
        check_vma=False,
    )
```

profile of v0, /device:TPU:2, one launch (start us, length us, event | category | flops | bytes accessed | tf_op | source)
XLA Modules:
  0.0 875.8 jit_solution(191999634789803929)
XLA Ops:
  14.3 13.6 %all_gather.15 = bf16[1,512,512]{2,1,0:T(8,128)(2,1)S(1)} all-gather(bf16[1,128,512]{2,1,0:T(8,128)(2,1)} %param.35), channel_id=1, replica_groups=mesh['dp'=4,'segment'=2,'band'=32] {'dp'}, dimensions={1}, use_global_device_ids=true | all-gather | bytes 655360 | tf_op jit(solution)/shard_map/all_gather | solution.py:190
  27.9 7.6 all_gather.13
  38.2 32.2 %all-gather.5.cloned.1.call-done = bf16[1,512,1536]{2,1,0:T(8,128)(2,1)} async-done(((bf16[1,128,1536]{2,1,0:T(8,128)(2,1)}), bf16[1,512,1536]{2,1,0:T(8,128)(2,1)}) %all-gather.5.cloned.1.call-update) | async-done | bytes 1572880 | tf_op jit(solution)/shard_map/all_gather | solution.py:189
  76.2 116.6 %while.103 = (s32[]{:T(128)}, bf16[2,8,16,512]{3,2,1,0:T(8,128)(2,1)}, bf16[2,8,16,1024]{3,2,1,0:T(8,128)(2,1)}, f32[2,8,16,512]{3,2,1,0:T(8,128)}, f32[2,8,16,1...) while((s32[]{:T(128)}, ...), condition=%wide.region_9.10_spmd, body=%wide.region_0.9_spmd.sunk | while | flops 477448448 | bytes 26721116 | solution.py:299
  77.2 5.2 conditional.18
  84.5 5.2 collective-permute-start.1
  103.1 27.5 %conditional.19 = (bf16[8,16,512]{2,1,0:T(8,128)(2,1)}, bf16[8,16,512]{2,1,0:T(8,128)(2,1)}) conditional(s32[]{:T(128)} %convert_element_type.561, () %tuple.323, (bf16[16,16,1024]{2,1,0:T(8,128)(2,1)}, pred[2,16,16]{2,1,0:T(8,128)(4,1)S(1)}, s32[]{:T(128)}, bf16[8,16,512]{2,1,0:T(8,128)(2,1)S(1)}, bf16[512,512]{1,0:T(8,128)(2,1)S(1)}, ...), branch_computations={%region_5.5_spmd, %region_6.8_spmd} | conditional | flops 137315840 | bytes 8476452 | solution.py:85
  135.4 5.2 conditional.18
  142.7 5.2 collective-permute-start.1
  161.4 27.5 %conditional.19 = (bf16[8,16,512]{2,1,0:T(8,128)(2,1)}, bf16[8,16,512]{2,1,0:T(8,128)(2,1)}) conditional(s32[]{:T(128)} %convert_element_type.561, () %tuple.323, (bf16[16,16,1024]{2,1,0:T(8,128)(2,1)}, pred[2,16,16]{2,1,0:T(8,128)(4,1)S(1)}, s32[]{:T(128)}, bf16[8,16,512]{2,1,0:T(8,128)(2,1)S(1)}, bf16[512,512]{1,0:T(8,128)(2,1)S(1)}, ...), branch_computations={%region_5.5_spmd, %region_6.8_spmd} | conditional | flops 137315840 | bytes 8476452 | solution.py:85
  194.7 54.8 %while.104 = (s32[]{:T(128)}, bf16[2,8,16,512]{3,2,1,0:T(8,128)(2,1)}, bf16[2,8,16,1024]{3,2,1,0:T(8,128)(2,1)}, f32[2,8,16,512]{3,2,1,0:T(8,128)}, f32[2,8,16,1...) while((s32[]{:T(128)}, ...), condition=%wide.region_19.20_spmd, body=%wide.region_10.19_spmd.sunk | while | flops 477448448 | bytes 26721116 | solution.py:303
  199.2 5.2 collective-permute-start.3
  226.6 5.2 collective-permute-start.3
  250.3 60.6 %while.106 = (s32[]{:T(128)}, bf16[2,8,16,512]{3,2,1,0:T(8,128)(2,1)}, f32[1024,512]{1,0:T(8,128)}, f32[512,1536]{1,0:T(8,128)}, f32[512,512]{1,0:T(8,128)}, /*i...) while((s32[]{:T(128)}, ...), condition=%wide.region_33.34_spmd.clone, body=%wide.region_20.33_spmd.clone.sunk | while | flops 992495872 | bytes 121524072 | solution.py:312
  255.1 4.3 collective-permute-start.6
  284.2 6.7 collective-permute-start.6
  303.3 4.3 select_add_fusion.8
  310.9 143.5 %collective-permute-start.11 = (bf16[2,8,16,512]{3,2,1,0:T(8,128)(2,1)}, bf16[2,8,16,512]{3,2,1,0:T(8,128)(2,1)S(1)}, u32[]{:S(2)}, u32[]{:S(2)}) collective-permute-start(bf16[2,8,16,512]{3,2,1,0:T(8,128)(2,1)} %get-tuple-element.2101), channel_id=1, source_target_pairs={{0,32},{32,0},{1,33},{33,1},{2,34},{34,2},{3,35},{35,3},{4,36},{36... | collective-permute-start | bytes 786440 | tf_op jit(solution)/shard_map/ppermute | solution.py:30
  455.8 131.6 %while.105 = (s32[]{:T(128)}, f32[1024,512]{1,0:T(8,128)}, f32[512,1536]{1,0:T(8,128)}, f32[512,512]{1,0:T(8,128)}, f32[512]{0:T(512)}, /*index=5*/s32[]{:T(128)...) while((s32[]{:T(128)}, f32[1024,512]{1,0:T(8,128)}, ...), condition=%wide.region_47.48_spmd, body=%wide.region_34.47_spmd.sunk | while | flops 856311552 | bytes 123788608 | solution.py:319
  456.6 35.0 %conditional.22 = (bf16[8,16,512]{2,1,0:T(8,128)(2,1)}, bf16[16,16,1024]{2,1,0:T(8,128)(2,1)}, f32[512,512]{1,0:T(8,128)}) conditional(s32[]{:T(128)} %convert_element_type.565, () %tuple.339, (pred[2,16,16]{2,1,0:T(8,128)(4,1)S(1)}, s32[]{:T(128)}, bf16[8,16,512]{2,1,0:T(8,128)(2,1)}, bf16[512,512]{1,0:T(8,128)(2,1)S(1)}, ...), branch_computations={%region_35.35_spmd, %region_36.41_spmd} | conditional | flops 316294400 | bytes 26212748 | solution.py:85
  492.6 6.2 collective-permute-start.4
  506.9 6.1 conditional.23
  514.7 4.3 add.947
  522.9 35.0 %conditional.22 = (bf16[8,16,512]{2,1,0:T(8,128)(2,1)}, bf16[16,16,1024]{2,1,0:T(8,128)(2,1)}, f32[512,512]{1,0:T(8,128)}) conditional(s32[]{:T(128)} %convert_element_type.565, () %tuple.339, (pred[2,16,16]{2,1,0:T(8,128)(4,1)S(1)}, s32[]{:T(128)}, bf16[8,16,512]{2,1,0:T(8,128)(2,1)}, bf16[512,512]{1,0:T(8,128)(2,1)S(1)}, ...), branch_computations={%region_35.35_spmd, %region_36.41_spmd} | conditional | flops 316294400 | bytes 26212748 | solution.py:85
  572.2 6.1 conditional.23
  580.0 4.3 add.947
  596.6 27.5 %reduce-scatter.11.cloned.1.call-done = bf16[1,128,512]{2,1,0:T(8,128)(2,1)} async-done(((bf16[1,512,512]{2,1,0:T(8,128)(2,1)}), bf16[1,128,512]{2,1,0:T(8,128)(2,1)}) %reduce-scatter.11.cloned.1.call-update) | async-done | bytes 131088 | tf_op jit(solution)/shard_map/reduce_scatter | solution.py:330
  624.1 28.4 %reduce-scatter.7.cloned.1.call-done = bf16[1,256,512]{2,1,0:T(8,128)(2,1)} async-done(((bf16[1,1024,512]{2,1,0:T(8,128)(2,1)}), bf16[1,256,512]{2,1,0:T(8,128)(2,1)}) %reduce-scatter.7.cloned.1.call-update) | async-done | bytes 262160 | tf_op jit(solution)/shard_map/reduce_scatter | solution.py:324
  652.5 31.1 %reduce-scatter.9.cloned.1.call-done = bf16[1,128,1536]{2,1,0:T(8,128)(2,1)} async-done(((bf16[1,512,1536]{2,1,0:T(8,128)(2,1)}), bf16[1,128,1536]{2,1,0:T(8,128)(2,1)}) %reduce-scatter.9.cloned.1.call-update) | async-done | bytes 393232 | tf_op jit(solution)/shard_map/reduce_scatter | solution.py:327
  683.6 25.3 %reduce-scatter.13.cloned.1.call-done = bf16[128,1]{1,0:T(8,128)(2,1)} async-done(((bf16[512,1]{1,0:T(8,128)(2,1)}), bf16[128,1]{1,0:T(8,128)(2,1)}) %reduce-scatter.13.cloned.1.call-update) | async-done | bytes 272
  709.8 75.3 %psum.31 = bf16[1,128]{1,0:T(2,128)(2,1)S(1)} all-reduce(bf16[1,128]{1,0:T(2,128)(2,1)S(1)} %copy.91), channel_id=1, replica_groups=mesh['dp'=4,'segment'=2,'band'=32] {'band'}, use_global_device_ids=true, to_apply=%region_55.56 | all-reduce | flops 128 | bytes 512 | tf_op jit(solution)/shard_map/psum | solution.py:341
  785.6 77.6 %all-reduce.11.cloned.1.call-done = (bf16[1,256,512]{2,1,0:T(8,128)(2,1)}, bf16[1,128,1536]{2,1,0:T(8,128)(2,1)}, bf16[1,128,512]{2,1,0:T(8,128)(2,1)}) async-done(((bf16[1,256,512]{2,1,0:T(8,128)(2,1)}, bf16[1,128,1536]{2,1,0:T(8,128)(2,1)}, bf16[1,128,512]{2,1,0:T(8,128)(2,1)}), (bf16[1,256,512]{2,1,0:T(8,128)(2,1)}, bf16[1,128,1536]{2,1,0:T(8,128)(2,1)}, ...) | async-done | bytes 786448 | tf_op jit(solution)/shard_map/psum | solution.py:338
  (498 shorter events, 359.9 us)
Async XLA Ops:
  7.2 31.1 %all-gather.3.cloned.1.call-start = ((), (), s32[]{:S(2)}) async-start(), calls=%async_computation.4 | async-start | bytes 1310720 | tf_op jit(solution)/shard_map/all_gather | solution.py:188
  7.9 62.5 %all-gather.5.cloned.1.call-start = ((), (), s32[]{:S(2)}) async-start(), calls=%async_computation.5 | async-start | bytes 1966080 | tf_op jit(solution)/shard_map/all_gather | solution.py:189
  8.6 615.4 %reduce-scatter.11.cloned.1.call-start = ((), (), s32[]{:S(2)}) async-start(), calls=%async_computation.8 | async-start | bytes 655360 | tf_op jit(solution)/shard_map/reduce_scatter | solution.py:330
  9.5 26.0 %collective-permute-start.8 = (s32[2,4,16]{2,1,0:T(4,128)S(1)}, s32[2,4,16]{2,1,0:T(4,128)S(1)}, u32[]{:S(2)}, u32[]{:S(2)}) collective-permute-start(s32[2,4,16]{2,1,0:T(4,128)S(1)} %get-tuple-element.2527), channel_id=1, source_target_pairs={{0,1},{1,2},{2,3},{3,4},{4,5},{5,6},{6,7},{7,8},{8,9},{9,10},{10,1... | collective-permute-start | bytes 1544 | tf_op jit(solution)/shard_map/ppermute | solution.py:23
  12.9 22.5 %collective-permute-start.9 = (s32[2,4,16]{2,1,0:T(4,128)S(1)}, s32[2,4,16]{2,1,0:T(4,128)S(1)}, u32[]{:S(2)}, u32[]{:S(2)}) collective-permute-start(s32[2,4,16]{2,1,0:T(4,128)S(1)} %get-tuple-element.2528), channel_id=1, source_target_pairs={{1,0},{2,1},{3,2},{4,3},{5,4},{6,5},{7,6},{8,7},{9,8},{10,9},{11,1... | collective-permute-start | bytes 1544 | tf_op jit(solution)/shard_map/ppermute | solution.py:24
  38.2 38.0 %copy-start.9 = (bf16[1,1024,512]{2,1,0:T(8,128)(2,1)S(1)}, bf16[1,1024,512]{2,1,0:T(8,128)(2,1)}, u32[]{:S(2)}) copy-start(bf16[1,1024,512]{2,1,0:T(8,128)(2,1)} %all-gather.3.cloned.1.call-done) | copy-start | bytes 3145732
  82.4 16.3 %copy-start.31 = (bf16[2,8,16,512]{3,2,1,0:T(8,128)(2,1)S(1)}, bf16[2,8,16,512]{3,2,1,0:T(8,128)(2,1)}, u32[]{:S(2)}) copy-start(bf16[2,8,16,512]{3,2,1,0:T(8,128)(2,1)} %get-tuple-element.3160) | copy-start | bytes 786436 | tf_op jit(solution)/shard_map/while
  83.2 18.0 %collective-permute-start = (bf16[4,16,1024]{2,1,0:T(8,128)(2,1)}, bf16[4,16,1024]{2,1,0:T(8,128)(2,1)}, u32[]{:S(2)}, u32[]{:S(2)}) collective-permute-start(bf16[4,16,1024]{2,1,0:T(8,128)(2,1)} %get-tuple-element.2975), channel_id=1, source_target_pairs={{1,0},{2,1},{3,2},{4,3},{5,4},{6,5},{7,6},{8,7},{9,8},{10,9},{11,1... | collective-permute-start | bytes 393224 | tf_op jit(solution)/shard_map/while/body/eval_jaxpr/ppermute | solution.py:24
  84.5 16.8 %collective-permute-start.1 = (bf16[4,16,1024]{2,1,0:T(8,128)(2,1)}, bf16[4,16,1024]{2,1,0:T(8,128)(2,1)}, u32[]{:S(2)}, u32[]{:S(2)}) collective-permute-start(bf16[4,16,1024]{2,1,0:T(8,128)(2,1)} %get-tuple-element.2976), channel_id=1, source_target_pairs={{0,1},{1,2},{2,3},{3,4},{4,5},{5,6},{6,7},{7,8},{8,9},{9,10},{10,1... | collective-permute-start | bytes 393224 | tf_op jit(solution)/shard_map/while/body/eval_jaxpr/ppermute | solution.py:23
  140.7 16.3 %copy-start.31 = (bf16[2,8,16,512]{3,2,1,0:T(8,128)(2,1)S(1)}, bf16[2,8,16,512]{3,2,1,0:T(8,128)(2,1)}, u32[]{:S(2)}) copy-start(bf16[2,8,16,512]{3,2,1,0:T(8,128)(2,1)} %get-tuple-element.3160) | copy-start | bytes 786436 | tf_op jit(solution)/shard_map/while
  141.5 18.0 %collective-permute-start = (bf16[4,16,1024]{2,1,0:T(8,128)(2,1)}, bf16[4,16,1024]{2,1,0:T(8,128)(2,1)}, u32[]{:S(2)}, u32[]{:S(2)}) collective-permute-start(bf16[4,16,1024]{2,1,0:T(8,128)(2,1)} %get-tuple-element.2975), channel_id=1, source_target_pairs={{1,0},{2,1},{3,2},{4,3},{5,4},{6,5},{7,6},{8,7},{9,8},{10,9},{11,1... | collective-permute-start | bytes 393224 | tf_op jit(solution)/shard_map/while/body/eval_jaxpr/ppermute | solution.py:24
  142.7 16.8 %collective-permute-start.1 = (bf16[4,16,1024]{2,1,0:T(8,128)(2,1)}, bf16[4,16,1024]{2,1,0:T(8,128)(2,1)}, u32[]{:S(2)}, u32[]{:S(2)}) collective-permute-start(bf16[4,16,1024]{2,1,0:T(8,128)(2,1)} %get-tuple-element.2976), channel_id=1, source_target_pairs={{0,1},{1,2},{2,3},{3,4},{4,5},{5,6},{6,7},{7,8},{8,9},{9,10},{10,1... | collective-permute-start | bytes 393224 | tf_op jit(solution)/shard_map/while/body/eval_jaxpr/ppermute | solution.py:23
  192.8 1.9 collective-permute-start.10
  197.9 17.1 %collective-permute-start.2 = (bf16[4,16,1024]{2,1,0:T(8,128)(2,1)}, bf16[4,16,1024]{2,1,0:T(8,128)(2,1)}, u32[]{:S(2)}, u32[]{:S(2)}) collective-permute-start(bf16[4,16,1024]{2,1,0:T(8,128)(2,1)} %get-tuple-element.3006), channel_id=1, source_target_pairs={{1,0},{2,1},{3,2},{4,3},{5,4},{6,5},{7,6},{8,7},{9,8},{10,9},{11,1... | collective-permute-start | bytes 393224 | tf_op jit(solution)/shard_map/while/body/eval_jaxpr/ppermute | solution.py:24
  199.2 15.8 %collective-permute-start.3 = (bf16[4,16,1024]{2,1,0:T(8,128)(2,1)}, bf16[4,16,1024]{2,1,0:T(8,128)(2,1)}, u32[]{:S(2)}, u32[]{:S(2)}) collective-permute-start(bf16[4,16,1024]{2,1,0:T(8,128)(2,1)} %get-tuple-element.3007), channel_id=1, source_target_pairs={{0,1},{1,2},{2,3},{3,4},{4,5},{5,6},{6,7},{7,8},{8,9},{9,10},{10,1... | collective-permute-start | bytes 393224 | tf_op jit(solution)/shard_map/while/body/eval_jaxpr/ppermute | solution.py:23
  225.3 17.1 %collective-permute-start.2 = (bf16[4,16,1024]{2,1,0:T(8,128)(2,1)}, bf16[4,16,1024]{2,1,0:T(8,128)(2,1)}, u32[]{:S(2)}, u32[]{:S(2)}) collective-permute-start(bf16[4,16,1024]{2,1,0:T(8,128)(2,1)} %get-tuple-element.3006), channel_id=1, source_target_pairs={{1,0},{2,1},{3,2},{4,3},{5,4},{6,5},{7,6},{8,7},{9,8},{10,9},{11,1... | collective-permute-start | bytes 393224 | tf_op jit(solution)/shard_map/while/body/eval_jaxpr/ppermute | solution.py:24
  226.6 15.8 %collective-permute-start.3 = (bf16[4,16,1024]{2,1,0:T(8,128)(2,1)}, bf16[4,16,1024]{2,1,0:T(8,128)(2,1)}, u32[]{:S(2)}, u32[]{:S(2)}) collective-permute-start(bf16[4,16,1024]{2,1,0:T(8,128)(2,1)} %get-tuple-element.3007), channel_id=1, source_target_pairs={{0,1},{1,2},{2,3},{3,4},{4,5},{5,6},{6,7},{7,8},{8,9},{9,10},{10,1... | collective-permute-start | bytes 393224 | tf_op jit(solution)/shard_map/while/body/eval_jaxpr/ppermute | solution.py:23
  255.1 11.4 %collective-permute-start.6 = (bf16[4,16,1024]{2,1,0:T(8,128)(2,1)}, bf16[4,16,1024]{2,1,0:T(8,128)(2,1)}, u32[]{:S(2)}, u32[]{:S(2)}) collective-permute-start(bf16[4,16,1024]{2,1,0:T(8,128)(2,1)} %get-tuple-element.3072), channel_id=1, source_target_pairs={{0,1},{1,2},{2,3},{3,4},{4,5},{5,6},{6,7},{7,8},{8,9},{9,10},{10,1... | collective-permute-start | bytes 393224 | tf_op jit(solution)/shard_map/while/body/eval_jaxpr/ppermute | solution.py:23
  259.4 8.4 collective-permute-start.7
  284.2 14.1 %collective-permute-start.6 = (bf16[4,16,1024]{2,1,0:T(8,128)(2,1)}, bf16[4,16,1024]{2,1,0:T(8,128)(2,1)}, u32[]{:S(2)}, u32[]{:S(2)}) collective-permute-start(bf16[4,16,1024]{2,1,0:T(8,128)(2,1)} %get-tuple-element.3072), channel_id=1, source_target_pairs={{0,1},{1,2},{2,3},{3,4},{4,5},{5,6},{6,7},{7,8},{8,9},{9,10},{10,1... | collective-permute-start | bytes 393224 | tf_op jit(solution)/shard_map/while/body/eval_jaxpr/ppermute | solution.py:23
  290.9 7.4 collective-permute-start.7
  310.9 144.9 %collective-permute-start.11 = (bf16[2,8,16,512]{3,2,1,0:T(8,128)(2,1)}, bf16[2,8,16,512]{3,2,1,0:T(8,128)(2,1)S(1)}, u32[]{:S(2)}, u32[]{:S(2)}) collective-permute-start(bf16[2,8,16,512]{3,2,1,0:T(8,128)(2,1)} %get-tuple-element.2101), channel_id=1, source_target_pairs={{0,32},{32,0},{1,33},{33,1},{2,34},{34,2},{3,35},{35,3},{4,36},{36... | collective-permute-start | bytes 786440 | tf_op jit(solution)/shard_map/ppermute | solution.py:30
  456.6 43.5 %copy-start.10 = (f32[512,512]{1,0:T(8,128)S(1)}, f32[512,512]{1,0:T(8,128)}, u32[]{:S(2)}) copy-start(f32[512,512]{1,0:T(8,128)} %get-tuple-element.3359) | copy-start | bytes 3145732 | tf_op jit(solution)/shard_map/while
  492.6 10.3 %collective-permute-start.4 = (bf16[4,16,1024]{2,1,0:T(8,128)(2,1)S(1)}, bf16[4,16,1024]{2,1,0:T(8,128)(2,1)}, u32[]{:S(2)}, u32[]{:S(2)}) collective-permute-start(bf16[4,16,1024]{2,1,0:T(8,128)(2,1)S(1)} %get-tuple-element.3040), channel_id=1, source_target_pairs={{0,1},{1,2},{2,3},{3,4},{4,5},{5,6},{6,7},{7,8},{8,9},{9,10},{10,1... | collective-permute-start | bytes 393224 | tf_op jit(solution)/shard_map/while/body/eval_jaxpr/ppermute | solution.py:23
  498.8 7.0 collective-permute-start.5
  522.9 41.3 %copy-start.10 = (f32[512,512]{1,0:T(8,128)S(1)}, f32[512,512]{1,0:T(8,128)}, u32[]{:S(2)}) copy-start(f32[512,512]{1,0:T(8,128)} %get-tuple-element.3359) | copy-start | bytes 3145732 | tf_op jit(solution)/shard_map/while
  558.9 8.2 collective-permute-start.4
  562.9 8.1 collective-permute-start.5
  589.5 62.9 %reduce-scatter.7.cloned.1.call-start = ((), (), s32[]{:S(2)}) async-start(), calls=%async_computation.6 | async-start | bytes 1310720 | tf_op jit(solution)/shard_map/reduce_scatter | solution.py:324
  592.4 91.3 %reduce-scatter.9.cloned.1.call-start = ((), (), s32[]{:S(2)}) async-start(), calls=%async_computation.7 | async-start | bytes 1966080 | tf_op jit(solution)/shard_map/reduce_scatter | solution.py:327
  595.7 113.3 %reduce-scatter.13.cloned.1.call-start = ((), (), s32[]{:S(2)}) async-start(), calls=%async_computation.9 | async-start | bytes 163840
  596.5 266.7 %all-reduce.11.cloned.1.call-start = ((), (), s32[]{:S(2)}) async-start(), calls=%async_computation.10 | async-start | bytes 1572864 | tf_op jit(solution)/shard_map/psum | solution.py:338
  (64 other events, 277.0 us)
Sparse Core Ops, SparseCore 0:
  9.8 28.3 all-gather.2
  40.0 30.3 all-gather.4
  589.7 34.3 reduce-scatter.10
  626.5 25.9 reduce-scatter.6
  655.0 28.5 reduce-scatter.8
  686.7 22.2 reduce-scatter.12
  712.6 150.6 all-reduce.10
where the time goes:
time: 888 us; the launch traced here: 876 us
  waiting for transfers between devices  237 us (27%)
  starting transfers between devices  201 us (23%)
  local copies, waits for them, and re-layouts  166 us (19%)
  other arithmetic  116 us (13%)
  blocking collectives  96.5 us (11%)
  matrix products  42.6 us (5%)
  between operations  14.6 us (2%)
    ppermute x2, starting transfers between devices, partner(): lax.ppermute(shard, axis, [(i, i ^ 1 << distance) for i in range(lax.axis...  144 us
    psum x1, waiting for transfers between devices, body(): lax.psum(merge_part_sum.astype(jnp.bfloat16), 'band').astype(jnp.float32)  77.6 us
    psum x1, blocking collectives, body(): lax.psum(gain_part_sum.astype(jnp.bfloat16), 'band').astype(jnp.float32)  75.3 us
    ppermute x9, starting transfers between devices, padded(): before = lax.ppermute(last, axis, up)  45.6 us
    slice x20, local copies, waits for them, and re-layouts, attend(): key_pairs = jnp.concatenate([kv_blocks[:-1], kv_blocks[1:]], axis=1)  38.4 us
    all_gather x1, waiting for transfers between devices, body(): lax.all_gather(qkv_weight, 'dp', axis=1, tiled=True)  32.2 us
    reduce_scatter x1, waiting for transfers between devices, body(): lax.psum_scatter(grad_sums[1][None].astype(jnp.bfloat16), 'dp', scatter_d...  31.1 us
    dynamic_update_slice x26, other arithmetic, place_one(): lax.dynamic_update_index_in_dim(buffer, jnp.where(active, new_value, curr...  30.9 us
  transfers between devices with their start and end apart: 27, of which 12 were waited for; matrix products, arithmetic and copies ran while one was open for 8% of the time, Pallas kernels for 0%

commit v1 on v0

--- a/solution.py
+++ b/solution.py
@@ -335,7 +335,9 @@
         ).astype(jnp.float32),
     )
     merge_grad, qkv_grad, out_grad, gain_grad = (
-        lax.psum(merge_part_sum.astype(jnp.bfloat16), "band").astype(jnp.float32),
+        jnp.sum(lax.all_gather(merge_part_sum.astype(jnp.bfloat16), "band"), axis=0).astype(
+            jnp.float32
+        ),
         lax.psum(qkv_part_sum.astype(jnp.bfloat16), "band").astype(jnp.float32),
         lax.psum(out_part_sum.astype(jnp.bfloat16), "band").astype(jnp.float32),
         lax.psum(gain_part_sum.astype(jnp.bfloat16), "band").astype(jnp.float32),

time: 888 us -> 985 us (1.11)
  waiting for transfers between devices: 237 us -> 332 us
    all_gather x0 -> x1, waiting for transfers between devices: none -> 94.8 us  [body(): lax.all_gather(merge_part_sum.astype(jnp.bfloat16), 'band')]
    unnamed x8 -> x9, waiting for transfers between devices: 26.8 us -> 27.3 us
  transfers between devices with their start and end apart: 27 -> 28, of which waited for: 12 -> 13; matrix products, arithmetic and copies ran while one was open for 8% -> 7% of each run, Pallas kernels for 0% -> 0%
where the time goes in v1:
time: 985 us; the launch traced here: 972 us
  waiting for transfers between devices  332 us (34%)
  starting transfers between devices  201 us (20%)
  local copies, waits for them, and re-layouts  166 us (17%)
  other arithmetic  118 us (12%)
  blocking collectives  96.4 us (10%)
  matrix products  42.5 us (4%)
  between operations  14.7 us (1%)
    ppermute x2, starting transfers between devices, partner(): lax.ppermute(shard, axis, [(i, i ^ 1 << distance) for i in range(lax.axis...  143 us
    all_gather x1, waiting for transfers between devices, body(): lax.all_gather(merge_part_sum.astype(jnp.bfloat16), 'band')  94.8 us
    psum x1, waiting for transfers between devices, body(): lax.psum(qkv_part_sum.astype(jnp.bfloat16), 'band').astype(jnp.float32)  76 us
    psum x1, blocking collectives, body(): lax.psum(gain_part_sum.astype(jnp.bfloat16), 'band').astype(jnp.float32)  75.2 us
    ppermute x9, starting transfers between devices, padded(): before = lax.ppermute(last, axis, up)  45.6 us
    slice x20, local copies, waits for them, and re-layouts, attend(): key_pairs = jnp.concatenate([kv_blocks[:-1], kv_blocks[1:]], axis=1)  38.3 us
    all_gather x1, waiting for transfers between devices, body(): lax.all_gather(qkv_weight, 'dp', axis=1, tiled=True)  32.2 us
    reduce_scatter x1, waiting for transfers between devices, body(): lax.psum_scatter(grad_sums[1][None].astype(jnp.bfloat16), 'dp', scatter_d...  31.1 us
  transfers between devices with their start and end apart: 28, of which 13 were waited for; matrix products, arithmetic and copies ran while one was open for 7% of the time, Pallas kernels for 0%

profile of v1, /device:TPU:2, one launch (start us, length us, event | category | flops | bytes accessed | tf_op | source)
XLA Modules:
  0.0 972.2 jit_solution(5336341358042183070)
XLA Ops:
  14.3 13.6 %all_gather.21 = bf16[1,512,512]{2,1,0:T(8,128)(2,1)S(1)} all-gather(bf16[1,128,512]{2,1,0:T(8,128)(2,1)} %param.35), channel_id=1, replica_groups=mesh['dp'=4,'segment'=2,'band'=32] {'dp'}, dimensions={1}, use_global_device_ids=true | all-gather | bytes 655360 | tf_op jit(solution)/shard_map/all_gather | solution.py:190
  27.9 7.6 all_gather.19
  38.2 32.2 %all-gather.7.cloned.1.call-done = bf16[1,512,1536]{2,1,0:T(8,128)(2,1)} async-done(((bf16[1,128,1536]{2,1,0:T(8,128)(2,1)}), bf16[1,512,1536]{2,1,0:T(8,128)(2,1)}) %all-gather.7.cloned.1.call-update) | async-done | bytes 1572880 | tf_op jit(solution)/shard_map/all_gather | solution.py:189
  76.2 116.5 %while.103 = (s32[]{:T(128)}, bf16[2,8,16,512]{3,2,1,0:T(8,128)(2,1)}, bf16[2,8,16,1024]{3,2,1,0:T(8,128)(2,1)}, f32[2,8,16,512]{3,2,1,0:T(8,128)}, f32[2,8,16,1...) while((s32[]{:T(128)}, ...), condition=%wide.region_9.10_spmd, body=%wide.region_0.9_spmd.sunk | while | flops 477448448 | bytes 26721116 | solution.py:299
  77.2 5.2 conditional.18
  84.4 5.2 collective-permute-start.1
  103.0 27.4 %conditional.19 = (bf16[8,16,512]{2,1,0:T(8,128)(2,1)}, bf16[8,16,512]{2,1,0:T(8,128)(2,1)}) conditional(s32[]{:T(128)} %convert_element_type.576, () %tuple.323, (bf16[16,16,1024]{2,1,0:T(8,128)(2,1)}, pred[2,16,16]{2,1,0:T(8,128)(4,1)S(1)}, s32[]{:T(128)}, bf16[8,16,512]{2,1,0:T(8,128)(2,1)S(1)}, bf16[512,512]{1,0:T(8,128)(2,1)S(1)}, ...), branch_computations={%region_5.5_spmd, %region_6.8_spmd} | conditional | flops 137315840 | bytes 8476452 | solution.py:85
  135.4 5.2 conditional.18
  142.7 5.2 collective-permute-start.1
  161.2 27.4 %conditional.19 = (bf16[8,16,512]{2,1,0:T(8,128)(2,1)}, bf16[8,16,512]{2,1,0:T(8,128)(2,1)}) conditional(s32[]{:T(128)} %convert_element_type.576, () %tuple.323, (bf16[16,16,1024]{2,1,0:T(8,128)(2,1)}, pred[2,16,16]{2,1,0:T(8,128)(4,1)S(1)}, s32[]{:T(128)}, bf16[8,16,512]{2,1,0:T(8,128)(2,1)S(1)}, bf16[512,512]{1,0:T(8,128)(2,1)S(1)}, ...), branch_computations={%region_5.5_spmd, %region_6.8_spmd} | conditional | flops 137315840 | bytes 8476452 | solution.py:85
  194.6 54.7 %while.104 = (s32[]{:T(128)}, bf16[2,8,16,512]{3,2,1,0:T(8,128)(2,1)}, bf16[2,8,16,1024]{3,2,1,0:T(8,128)(2,1)}, f32[2,8,16,512]{3,2,1,0:T(8,128)}, f32[2,8,16,1...) while((s32[]{:T(128)}, ...), condition=%wide.region_19.20_spmd, body=%wide.region_10.19_spmd.sunk | while | flops 477448448 | bytes 26721116 | solution.py:303
  199.0 5.2 collective-permute-start.3
  226.4 5.2 collective-permute-start.3
  250.0 60.7 %while.106 = (s32[]{:T(128)}, bf16[2,8,16,512]{3,2,1,0:T(8,128)(2,1)}, f32[1024,512]{1,0:T(8,128)}, f32[512,1536]{1,0:T(8,128)}, f32[512,512]{1,0:T(8,128)}, /*i...) while((s32[]{:T(128)}, ...), condition=%wide.region_33.34_spmd.clone, body=%wide.region_20.33_spmd.clone.sunk | while | flops 992495872 | bytes 121524072 | solution.py:312
  254.7 4.4 collective-permute-start.6
  283.9 6.7 collective-permute-start.6
  303.0 4.3 select_add_fusion.8
  310.7 143.3 %collective-permute-start.11 = (bf16[2,8,16,512]{3,2,1,0:T(8,128)(2,1)}, bf16[2,8,16,512]{3,2,1,0:T(8,128)(2,1)S(1)}, u32[]{:S(2)}, u32[]{:S(2)}) collective-permute-start(bf16[2,8,16,512]{3,2,1,0:T(8,128)(2,1)} %get-tuple-element.2101), channel_id=1, source_target_pairs={{0,32},{32,0},{1,33},{33,1},{2,34},{34,2},{3,35},{35,3},{4,36},{36... | collective-permute-start | bytes 786440 | tf_op jit(solution)/shard_map/ppermute | solution.py:30
  455.3 131.6 %while.105 = (s32[]{:T(128)}, f32[1024,512]{1,0:T(8,128)}, f32[512,1536]{1,0:T(8,128)}, f32[512,512]{1,0:T(8,128)}, f32[512]{0:T(512)}, /*index=5*/s32[]{:T(128)...) while((s32[]{:T(128)}, f32[1024,512]{1,0:T(8,128)}, ...), condition=%wide.region_47.48_spmd, body=%wide.region_34.47_spmd.sunk | while | flops 856311552 | bytes 123788608 | solution.py:319
  456.1 34.9 %conditional.22 = (bf16[8,16,512]{2,1,0:T(8,128)(2,1)}, bf16[16,16,1024]{2,1,0:T(8,128)(2,1)}, f32[512,512]{1,0:T(8,128)}) conditional(s32[]{:T(128)} %convert_element_type.580, () %tuple.339, (pred[2,16,16]{2,1,0:T(8,128)(4,1)S(1)}, s32[]{:T(128)}, bf16[8,16,512]{2,1,0:T(8,128)(2,1)}, bf16[512,512]{1,0:T(8,128)(2,1)S(1)}, ...), branch_computations={%region_35.35_spmd, %region_36.41_spmd} | conditional | flops 316294400 | bytes 26212748 | solution.py:85
  492.0 6.2 collective-permute-start.4
  506.2 6.1 conditional.23
  522.2 34.9 %conditional.22 = (bf16[8,16,512]{2,1,0:T(8,128)(2,1)}, bf16[16,16,1024]{2,1,0:T(8,128)(2,1)}, f32[512,512]{1,0:T(8,128)}) conditional(s32[]{:T(128)} %convert_element_type.580, () %tuple.339, (pred[2,16,16]{2,1,0:T(8,128)(4,1)S(1)}, s32[]{:T(128)}, bf16[8,16,512]{2,1,0:T(8,128)(2,1)}, bf16[512,512]{1,0:T(8,128)(2,1)S(1)}, ...), branch_computations={%region_35.35_spmd, %region_36.41_spmd} | conditional | flops 316294400 | bytes 26212748 | solution.py:85
  571.5 6.1 conditional.23
  594.7 28.9 %reduce-scatter.11.cloned.1.call-done = bf16[1,128,512]{2,1,0:T(8,128)(2,1)} async-done(((bf16[1,512,512]{2,1,0:T(8,128)(2,1)}), bf16[1,128,512]{2,1,0:T(8,128)(2,1)}) %reduce-scatter.11.cloned.1.call-update) | async-done | bytes 131088 | tf_op jit(solution)/shard_map/reduce_scatter | solution.py:330
  623.6 31.1 %reduce-scatter.9.cloned.1.call-done = bf16[1,128,1536]{2,1,0:T(8,128)(2,1)} async-done(((bf16[1,512,1536]{2,1,0:T(8,128)(2,1)}), bf16[1,128,1536]{2,1,0:T(8,128)(2,1)}) %reduce-scatter.9.cloned.1.call-update) | async-done | bytes 393232 | tf_op jit(solution)/shard_map/reduce_scatter | solution.py:327
  654.8 27.7 %reduce-scatter.7.cloned.1.call-done = bf16[1,256,512]{2,1,0:T(8,128)(2,1)} async-done(((bf16[1,1024,512]{2,1,0:T(8,128)(2,1)}), bf16[1,256,512]{2,1,0:T(8,128)(2,1)}) %reduce-scatter.7.cloned.1.call-update) | async-done | bytes 262160 | tf_op jit(solution)/shard_map/reduce_scatter | solution.py:324
  682.5 25.8 %reduce-scatter.13.cloned.1.call-done = bf16[128,1]{1,0:T(8,128)(2,1)} async-done(((bf16[512,1]{1,0:T(8,128)(2,1)}), bf16[128,1]{1,0:T(8,128)(2,1)}) %reduce-scatter.13.cloned.1.call-update) | async-done | bytes 272
  709.1 75.2 %psum.23 = bf16[1,128]{1,0:T(2,128)(2,1)S(1)} all-reduce(bf16[1,128]{1,0:T(2,128)(2,1)S(1)} %copy.91), channel_id=1, replica_groups=mesh['dp'=4,'segment'=2,'band'=32] {'band'}, use_global_device_ids=true, to_apply=%region_55.56 | all-reduce | flops 128 | bytes 512 | tf_op jit(solution)/shard_map/psum | solution.py:343
  784.9 76.0 %all-reduce.11.cloned.1.call-done = (bf16[1,128,1536]{2,1,0:T(8,128)(2,1)}, bf16[1,128,512]{2,1,0:T(8,128)(2,1)}) async-done(((bf16[1,128,1536]{2,1,0:T(8,128)(2,1)}, bf16[1,128,512]{2,1,0:T(8,128)(2,1)}), (bf16[1,128,1536]{2,1,0:T(8,128)(2,1)}, bf16[1,128,512]{2,1,0:T(8,128)(2,1)})) %all-reduce.11.cloned.1.call-update) | async-done | bytes 524304 | tf_op jit(solution)/shard_map/psum | solution.py:341
  864.5 94.8 %all-gather.9.cloned.1.call-done = bf16[32,256,512]{2,1,0:T(8,128)(2,1)} async-done(((bf16[1,256,512]{2,1,0:T(8,128)(2,1)}), bf16[32,256,512]{2,1,0:T(8,128)(2,1)}) %all-gather.9.cloned.1.call-update) | async-done | bytes 8388624 | tf_op jit(solution)/shard_map/all_gather | solution.py:338
  959.3 4.8 reduce.54
  (504 shorter events, 365.6 us)
Async XLA Ops:
  7.2 31.1 %all-gather.5.cloned.1.call-start = ((), (), s32[]{:S(2)}) async-start(), calls=%async_computation.4 | async-start | bytes 1310720 | tf_op jit(solution)/shard_map/all_gather | solution.py:188
  7.9 62.5 %all-gather.7.cloned.1.call-start = ((), (), s32[]{:S(2)}) async-start(), calls=%async_computation.5 | async-start | bytes 1966080 | tf_op jit(solution)/shard_map/all_gather | solution.py:189
  8.6 614.9 %reduce-scatter.11.cloned.1.call-start = ((), (), s32[]{:S(2)}) async-start(), calls=%async_computation.8 | async-start | bytes 655360 | tf_op jit(solution)/shard_map/reduce_scatter | solution.py:330
  9.5 26.0 %collective-permute-start.8 = (s32[2,4,16]{2,1,0:T(4,128)S(1)}, s32[2,4,16]{2,1,0:T(4,128)S(1)}, u32[]{:S(2)}, u32[]{:S(2)}) collective-permute-start(s32[2,4,16]{2,1,0:T(4,128)S(1)} %get-tuple-element.2526), channel_id=1, source_target_pairs={{0,1},{1,2},{2,3},{3,4},{4,5},{5,6},{6,7},{7,8},{8,9},{9,10},{10,1... | collective-permute-start | bytes 1544 | tf_op jit(solution)/shard_map/ppermute | solution.py:23
  12.9 22.5 %collective-permute-start.9 = (s32[2,4,16]{2,1,0:T(4,128)S(1)}, s32[2,4,16]{2,1,0:T(4,128)S(1)}, u32[]{:S(2)}, u32[]{:S(2)}) collective-permute-start(s32[2,4,16]{2,1,0:T(4,128)S(1)} %get-tuple-element.2527), channel_id=1, source_target_pairs={{1,0},{2,1},{3,2},{4,3},{5,4},{6,5},{7,6},{8,7},{9,8},{10,9},{11,1... | collective-permute-start | bytes 1544 | tf_op jit(solution)/shard_map/ppermute | solution.py:24
  38.2 38.0 %copy-start.10 = (bf16[1,1024,512]{2,1,0:T(8,128)(2,1)S(1)}, bf16[1,1024,512]{2,1,0:T(8,128)(2,1)}, u32[]{:S(2)}) copy-start(bf16[1,1024,512]{2,1,0:T(8,128)(2,1)} %all-gather.5.cloned.1.call-done) | copy-start | bytes 3145732
  82.4 16.3 %copy-start.32 = (bf16[2,8,16,512]{3,2,1,0:T(8,128)(2,1)S(1)}, bf16[2,8,16,512]{3,2,1,0:T(8,128)(2,1)}, u32[]{:S(2)}) copy-start(bf16[2,8,16,512]{3,2,1,0:T(8,128)(2,1)} %get-tuple-element.3159) | copy-start | bytes 786436 | tf_op jit(solution)/shard_map/while
  83.2 18.0 %collective-permute-start = (bf16[4,16,1024]{2,1,0:T(8,128)(2,1)}, bf16[4,16,1024]{2,1,0:T(8,128)(2,1)}, u32[]{:S(2)}, u32[]{:S(2)}) collective-permute-start(bf16[4,16,1024]{2,1,0:T(8,128)(2,1)} %get-tuple-element.2974), channel_id=1, source_target_pairs={{1,0},{2,1},{3,2},{4,3},{5,4},{6,5},{7,6},{8,7},{9,8},{10,9},{11,1... | collective-permute-start | bytes 393224 | tf_op jit(solution)/shard_map/while/body/eval_jaxpr/ppermute | solution.py:24
  84.4 16.7 %collective-permute-start.1 = (bf16[4,16,1024]{2,1,0:T(8,128)(2,1)}, bf16[4,16,1024]{2,1,0:T(8,128)(2,1)}, u32[]{:S(2)}, u32[]{:S(2)}) collective-permute-start(bf16[4,16,1024]{2,1,0:T(8,128)(2,1)} %get-tuple-element.2975), channel_id=1, source_target_pairs={{0,1},{1,2},{2,3},{3,4},{4,5},{5,6},{6,7},{7,8},{8,9},{9,10},{10,1... | collective-permute-start | bytes 393224 | tf_op jit(solution)/shard_map/while/body/eval_jaxpr/ppermute | solution.py:23
  141.4 18.0 %collective-permute-start = (bf16[4,16,1024]{2,1,0:T(8,128)(2,1)}, bf16[4,16,1024]{2,1,0:T(8,128)(2,1)}, u32[]{:S(2)}, u32[]{:S(2)}) collective-permute-start(bf16[4,16,1024]{2,1,0:T(8,128)(2,1)} %get-tuple-element.2974), channel_id=1, source_target_pairs={{1,0},{2,1},{3,2},{4,3},{5,4},{6,5},{7,6},{8,7},{9,8},{10,9},{11,1... | collective-permute-start | bytes 393224 | tf_op jit(solution)/shard_map/while/body/eval_jaxpr/ppermute | solution.py:24
  142.7 16.7 %collective-permute-start.1 = (bf16[4,16,1024]{2,1,0:T(8,128)(2,1)}, bf16[4,16,1024]{2,1,0:T(8,128)(2,1)}, u32[]{:S(2)}, u32[]{:S(2)}) collective-permute-start(bf16[4,16,1024]{2,1,0:T(8,128)(2,1)} %get-tuple-element.2975), channel_id=1, source_target_pairs={{0,1},{1,2},{2,3},{3,4},{4,5},{5,6},{6,7},{7,8},{8,9},{9,10},{10,1... | collective-permute-start | bytes 393224 | tf_op jit(solution)/shard_map/while/body/eval_jaxpr/ppermute | solution.py:23
  192.7 1.9 collective-permute-start.10
  197.7 17.1 %collective-permute-start.2 = (bf16[4,16,1024]{2,1,0:T(8,128)(2,1)}, bf16[4,16,1024]{2,1,0:T(8,128)(2,1)}, u32[]{:S(2)}, u32[]{:S(2)}) collective-permute-start(bf16[4,16,1024]{2,1,0:T(8,128)(2,1)} %get-tuple-element.3005), channel_id=1, source_target_pairs={{1,0},{2,1},{3,2},{4,3},{5,4},{6,5},{7,6},{8,7},{9,8},{10,9},{11,1... | collective-permute-start | bytes 393224 | tf_op jit(solution)/shard_map/while/body/eval_jaxpr/ppermute | solution.py:24
  199.0 15.8 %collective-permute-start.3 = (bf16[4,16,1024]{2,1,0:T(8,128)(2,1)}, bf16[4,16,1024]{2,1,0:T(8,128)(2,1)}, u32[]{:S(2)}, u32[]{:S(2)}) collective-permute-start(bf16[4,16,1024]{2,1,0:T(8,128)(2,1)} %get-tuple-element.3006), channel_id=1, source_target_pairs={{0,1},{1,2},{2,3},{3,4},{4,5},{5,6},{6,7},{7,8},{8,9},{9,10},{10,1... | collective-permute-start | bytes 393224 | tf_op jit(solution)/shard_map/while/body/eval_jaxpr/ppermute | solution.py:23
  225.1 17.1 %collective-permute-start.2 = (bf16[4,16,1024]{2,1,0:T(8,128)(2,1)}, bf16[4,16,1024]{2,1,0:T(8,128)(2,1)}, u32[]{:S(2)}, u32[]{:S(2)}) collective-permute-start(bf16[4,16,1024]{2,1,0:T(8,128)(2,1)} %get-tuple-element.3005), channel_id=1, source_target_pairs={{1,0},{2,1},{3,2},{4,3},{5,4},{6,5},{7,6},{8,7},{9,8},{10,9},{11,1... | collective-permute-start | bytes 393224 | tf_op jit(solution)/shard_map/while/body/eval_jaxpr/ppermute | solution.py:24
  226.4 15.8 %collective-permute-start.3 = (bf16[4,16,1024]{2,1,0:T(8,128)(2,1)}, bf16[4,16,1024]{2,1,0:T(8,128)(2,1)}, u32[]{:S(2)}, u32[]{:S(2)}) collective-permute-start(bf16[4,16,1024]{2,1,0:T(8,128)(2,1)} %get-tuple-element.3006), channel_id=1, source_target_pairs={{0,1},{1,2},{2,3},{3,4},{4,5},{5,6},{6,7},{7,8},{8,9},{9,10},{10,1... | collective-permute-start | bytes 393224 | tf_op jit(solution)/shard_map/while/body/eval_jaxpr/ppermute | solution.py:23
  254.7 11.4 %collective-permute-start.6 = (bf16[4,16,1024]{2,1,0:T(8,128)(2,1)}, bf16[4,16,1024]{2,1,0:T(8,128)(2,1)}, u32[]{:S(2)}, u32[]{:S(2)}) collective-permute-start(bf16[4,16,1024]{2,1,0:T(8,128)(2,1)} %get-tuple-element.3071), channel_id=1, source_target_pairs={{0,1},{1,2},{2,3},{3,4},{4,5},{5,6},{6,7},{7,8},{8,9},{9,10},{10,1... | collective-permute-start | bytes 393224 | tf_op jit(solution)/shard_map/while/body/eval_jaxpr/ppermute | solution.py:23
  259.1 8.4 collective-permute-start.7
  283.9 14.1 %collective-permute-start.6 = (bf16[4,16,1024]{2,1,0:T(8,128)(2,1)}, bf16[4,16,1024]{2,1,0:T(8,128)(2,1)}, u32[]{:S(2)}, u32[]{:S(2)}) collective-permute-start(bf16[4,16,1024]{2,1,0:T(8,128)(2,1)} %get-tuple-element.3071), channel_id=1, source_target_pairs={{0,1},{1,2},{2,3},{3,4},{4,5},{5,6},{6,7},{7,8},{8,9},{9,10},{10,1... | collective-permute-start | bytes 393224 | tf_op jit(solution)/shard_map/while/body/eval_jaxpr/ppermute | solution.py:23
  290.6 7.4 collective-permute-start.7
  310.7 144.6 %collective-permute-start.11 = (bf16[2,8,16,512]{3,2,1,0:T(8,128)(2,1)}, bf16[2,8,16,512]{3,2,1,0:T(8,128)(2,1)S(1)}, u32[]{:S(2)}, u32[]{:S(2)}) collective-permute-start(bf16[2,8,16,512]{3,2,1,0:T(8,128)(2,1)} %get-tuple-element.2101), channel_id=1, source_target_pairs={{0,32},{32,0},{1,33},{33,1},{2,34},{34,2},{3,35},{35,3},{4,36},{36... | collective-permute-start | bytes 786440 | tf_op jit(solution)/shard_map/ppermute | solution.py:30
  456.1 43.4 %copy-start.11 = (f32[512,512]{1,0:T(8,128)S(1)}, f32[512,512]{1,0:T(8,128)}, u32[]{:S(2)}) copy-start(f32[512,512]{1,0:T(8,128)} %get-tuple-element.3358) | copy-start | bytes 3145732 | tf_op jit(solution)/shard_map/while
  492.0 10.3 %collective-permute-start.4 = (bf16[4,16,1024]{2,1,0:T(8,128)(2,1)S(1)}, bf16[4,16,1024]{2,1,0:T(8,128)(2,1)}, u32[]{:S(2)}, u32[]{:S(2)}) collective-permute-start(bf16[4,16,1024]{2,1,0:T(8,128)(2,1)S(1)} %get-tuple-element.3039), channel_id=1, source_target_pairs={{0,1},{1,2},{2,3},{3,4},{4,5},{5,6},{6,7},{7,8},{8,9},{9,10},{10,1... | collective-permute-start | bytes 393224 | tf_op jit(solution)/shard_map/while/body/eval_jaxpr/ppermute | solution.py:23
  498.2 7.0 collective-permute-start.5
  522.2 41.3 %copy-start.11 = (f32[512,512]{1,0:T(8,128)S(1)}, f32[512,512]{1,0:T(8,128)}, u32[]{:S(2)}) copy-start(f32[512,512]{1,0:T(8,128)} %get-tuple-element.3358) | copy-start | bytes 3145732 | tf_op jit(solution)/shard_map/while
  558.2 8.2 collective-permute-start.4
  562.2 8.2 collective-permute-start.5
  589.0 65.7 %reduce-scatter.9.cloned.1.call-start = ((), (), s32[]{:S(2)}) async-start(), calls=%async_computation.7 | async-start | bytes 1966080 | tf_op jit(solution)/shard_map/reduce_scatter | solution.py:327
  592.5 89.9 %reduce-scatter.7.cloned.1.call-start = ((), (), s32[]{:S(2)}) async-start(), calls=%async_computation.6 | async-start | bytes 1310720 | tf_op jit(solution)/shard_map/reduce_scatter | solution.py:324
  593.7 114.6 %reduce-scatter.13.cloned.1.call-start = ((), (), s32[]{:S(2)}) async-start(), calls=%async_computation.10 | async-start | bytes 163840
  594.6 266.3 %all-reduce.11.cloned.1.call-start = ((), (), s32[]{:S(2)}) async-start(), calls=%async_computation.11 | async-start | bytes 1048576 | tf_op jit(solution)/shard_map/psum | solution.py:341
  654.7 304.6 %all-gather.9.cloned.1.call-start = ((), (), s32[]{:S(2)}) async-start(), calls=%async_computation.9 | async-start | bytes 8650752 | tf_op jit(solution)/shard_map/all_gather | solution.py:338
  (66 other events, 294.3 us)
Sparse Core Ops, SparseCore 0:
  9.8 28.3 all-gather.4
  40.0 30.3 all-gather.6
  589.2 34.3 reduce-scatter.10
  626.0 28.6 reduce-scatter.8
  657.1 25.2 reduce-scatter.6
  685.5 22.7 reduce-scatter.12
  711.7 149.1 all-reduce.10
  863.8 95.4 all-gather.8
